TPU v7x, 128 devices: a whole 4x4x4 slice. The times are simulated.
128 devices in a mesh: ctx: 16 (over y, z), kvh: 8 (over x, core).
Axes of the slice: x: 4, y: 4, z: 4, core: 2. Of those that a mesh axis runs over, the one named last changes fastest.
Arguments:
- query: bfloat16 [4, 4, 16384], P(None, None, 'kvh'), may hold values from -100 to 100
- new_kv: bfloat16 [2, 4, 4, 1024], P(None, None, None, 'kvh'), may hold values from -10 to 10
- kv_cache: bfloat16 [2, 4, 8, 16384, 128], P(None, None, 'kvh', 'ctx'), may hold values from -4 to 4
- lengths: int32 [4], replicated, may hold values from 2 to 16384, as said below
- residual: bfloat16 [4, 4, 16384], P(None, None, ('ctx', 'kvh')), may hold values from -6 to 6
- out_weight: bfloat16 [16384, 16384], P('kvh', 'ctx'), may hold values from -0.75 to 0.75
- norm_gain: float32 [16384], P(('ctx', 'kvh')), may hold values from 0.25 to 1.75
- gate_weight: bfloat16 [26624, 16384], P(('ctx', 'kvh')), may hold values from -0.046875 to 0.046875
- up_weight: bfloat16 [26624, 16384], P(('ctx', 'kvh')), may hold values from -0.046875 to 0.046875
- down_weight: bfloat16 [26624, 16384], P(('ctx', 'kvh')), may hold values from -0.125 to 0.125
Outputs:
- layer_out: bfloat16 [4, 4, 16384], P(None, None, ('ctx', 'kvh'))
Inputs may be any that keep to these rules, and one draw needn't show every extreme that they name: `lengths`: at least one sequence has exactly 16384 filled positions.
All inputs are finite; a program needn't handle non-finite values.
Results may differ from a plain program's by a relative error of at most 0.013.
Values may be sent and summed in bfloat16 or wider, within the bound.
A program may use at most 128 MiB of HBM per device.

v0:
```python
import math

import jax
import jax.numpy as jnp
from jax import lax
from jax.sharding import PartitionSpec as P

D = 16384


epsilon = 1e-05


def contract_rows(left, right):
    return lax.dot_general(
        left, right, (((1,), (1,)), ((), ())), preferred_element_type=jnp.float32
    )


def per_device(
    query,
    new_kv,
    kv_cache,
    lengths,
    residual,
    out_weight,
    norm_gain,
    gate_weight,
    up_weight,
    down_weight,
):
    step_count, batch_size, query_width = query.shape
    groups = kv_cache.shape[2]
    shard_len = kv_cache.shape[3]
    head_dim = kv_cache.shape[4]
    per_group = query_width // (groups * head_dim)
    scale = 1.0 / math.sqrt(head_dim)
    queries = query.reshape(step_count, batch_size, groups, per_group, head_dim)
    draft_keys = new_kv[0].reshape(step_count, batch_size, groups, head_dim)
    draft_values = new_kv[1].reshape(step_count, batch_size, groups, head_dim)
    cache_scores = (
        jnp.einsum("tbgjd,bgpd->tbgjp", queries, kv_cache[0], preferred_element_type=jnp.float32)
        * scale
    )
    draft_scores = (
        jnp.einsum("tbgjd,sbgd->tbgjs", queries, draft_keys, preferred_element_type=jnp.float32)
        * scale
    )
    ctx_index = lax.axis_index("ctx")
    position = ctx_index * shard_len + jnp.arange(shard_len, dtype=jnp.int32)
    cache_ok = (position[None, :] < lengths[:, None])[None, :, None, None, :]
    step_ids = jnp.arange(step_count, dtype=jnp.int32)
    draft_ok = (step_ids[None, :] <= step_ids[:, None]) & (ctx_index == 0)
    draft_ok = draft_ok[:, None, None, None, :]
    local_max = jnp.maximum(
        jnp.max(jnp.where(cache_ok, cache_scores, -1e30), axis=-1),
        jnp.max(jnp.where(draft_ok, draft_scores, -1e30), axis=-1),
    )
    highest = lax.pmax(local_max, "ctx")
    cache_weights = jnp.where(cache_ok, jnp.exp(cache_scores - highest[..., None]), 0.0)
    draft_weights = jnp.where(draft_ok, jnp.exp(draft_scores - highest[..., None]), 0.0)
    denominator = jnp.sum(cache_weights, axis=-1) + jnp.sum(draft_weights, axis=-1)
    numerator = jnp.einsum(
        "tbgjp,bgpd->tbgjd", cache_weights, kv_cache[1], preferred_element_type=jnp.float32
    )
    numerator = numerator + jnp.einsum(
        "tbgjs,sbgd->tbgjd", draft_weights, draft_values, preferred_element_type=jnp.float32
    )
    denominator, numerator = (denominator, numerator)
    denominator, numerator = lax.psum((denominator, numerator), "ctx")
    token_rows = step_count * batch_size
    attended = (
        (numerator / denominator[..., None]).astype(jnp.bfloat16).reshape(token_rows, query_width)
    )
    feat_local = residual.shape[2]
    residual_rows = residual.reshape(token_rows, feat_local).astype(jnp.float32)
    projected_block = jnp.dot(attended, out_weight, preferred_element_type=jnp.float32)
    projected = lax.psum_scatter(projected_block, "kvh", scatter_dimension=1, tiled=True)
    carried = (residual_rows + projected).astype(jnp.bfloat16)
    carried_wide = carried.astype(jnp.float32)
    squares = lax.psum(jnp.sum(carried_wide * carried_wide, axis=1), ("ctx", "kvh"))
    normed = (carried_wide * lax.rsqrt(squares[:, None] / D + epsilon) * norm_gain[None, :]).astype(
        jnp.bfloat16
    )
    piece = lax.all_gather(normed, ("ctx", "kvh"), axis=1, tiled=True)
    gate = contract_rows(piece, gate_weight)
    up_part = contract_rows(piece, up_weight)
    hidden = (jax.nn.silu(gate) * up_part).astype(jnp.bfloat16)
    down_block = jnp.dot(hidden, down_weight, preferred_element_type=jnp.float32)
    down = lax.psum_scatter(down_block, ("ctx", "kvh"), scatter_dimension=1, tiled=True)
    result = (carried_wide + down).astype(jnp.bfloat16)
    return result.reshape(step_count, batch_size, feat_local)


def solution(mesh):
    return jax.shard_map(
        per_device,
        mesh=mesh,
        in_specs=(
            P(None, None, "kvh"),
            P(None, None, None, "kvh"),
            P(None, None, "kvh", "ctx", None),
            P(),
            P(None, None, ("ctx", "kvh")),
            P("kvh", "ctx"),
            P(("ctx", "kvh")),
            P(("ctx", "kvh"), None),
            P(("ctx", "kvh"), None),
            P(("ctx", "kvh"), None),
        ),
        out_specs=P(None, None, ("ctx", "kvh")),
        check_vma=False,
    )
```

profile of v0, /device:TPU:1, one launch (start us, length us, event | category | flops | bytes accessed | tf_op | source)
XLA Modules:
  0.0 922.1 jit_solution(10084157453986377483)
XLA Ops:
  6.5 0.0 copy-start
  6.5 0.0 copy-start.1
  6.5 0.0 all-reduce.2.cloned.1.call-start
  6.6 0.7 fusion.37
  7.3 0.9 reshape.136
  8.2 0.7 broadcast_compare_fusion
  8.9 0.3 select_reduce_fusion.1
  9.2 1.8 select_reduce_fusion
  11.0 36.1 %pmax.7 = f32[4,4,16]{2,0,1:T(4,128)S(1)} all-reduce(f32[4,4,16]{2,0,1:T(4,128)S(1)} %max.16), channel_id=1, replica_groups=mesh['ctx'=16,'kvh'=8] {'ctx'}, use_global_device_ids=true, to_apply=%region_2.3 | all-reduce | flops 256 | bytes 2048 | tf_op jit(solution)/shard_map/pmax | solution.py:59
  47.1 1.6 fusion.4
  48.7 0.9 fusion.1
  49.7 0.0 all-reduce.2.cloned.1.call-update
  49.7 0.0 reduce-scatter.3.cloned.1.call-start
  49.7 0.3 fusion.7
  50.1 0.1 fusion.17
  50.2 29.1 %psum.22 = f32[4,4,16]{2,0,1:T(4,128)S(1)} all-reduce(f32[4,4,16]{2,0,1:T(4,128)S(1)} %add.66), channel_id=1, replica_groups=mesh['ctx'=16,'kvh'=8] {'ctx'}, use_global_device_ids=true, to_apply=%region_6.7 | all-reduce | flops 256 | bytes 2048 | tf_op jit(solution)/shard_map/psum | solution.py:70
  79.3 54.9 %all-reduce.2.cloned.1.call-done = f32[4,4,1,16,128]{4,3,0,1,2:T(8,128)} async-done(((f32[4,4,1,16,128]{4,3,0,1,2:T(8,128)}), f32[4,4,1,16,128]{4,3,0,1,2:T(8,128)}) %all-reduce.2.cloned.1.call-update) | async-done | bytes 131088 | tf_op jit(solution)/shard_map/psum | solution.py:70
  134.2 1.0 divide_convert_fusion
  135.2 3.5 fusion.11
  138.7 0.0 reduce-scatter.3.cloned.1.call-update
  138.7 0.0 reduce-scatter.5.cloned.1.call-start
  138.8 28.4 %reduce-scatter.3.cloned.1.call-done = f32[16,128]{1,0:T(8,128)} async-done(((f32[16,1024]{1,0:T(8,128)}), f32[16,128]{1,0:T(8,128)}) %reduce-scatter.3.cloned.1.call-update) | async-done | bytes 8208 | tf_op jit(solution)/shard_map/reduce_scatter | solution.py:78
  167.2 0.0 copy-done
  167.2 0.8 fusion.26
  168.0 67.5 %psum.23 = f32[16]{0:T(128)S(1)} all-reduce(f32[16]{0:T(128)S(1)} %get-tuple-element.5), channel_id=1, replica_groups=mesh['ctx'=16,'kvh'=8] {'ctx','kvh'}, use_global_device_ids=true, to_apply=%region_9.10 | all-reduce | flops 16 | bytes 128 | tf_op jit(solution)/shard_map/psum | solution.py:81
  235.5 0.0 copy-done.1
  235.5 0.1 fusion.28
  235.6 34.5 %all_gather.3 = bf16[16,16384]{1,0:T(8,128)(2,1)S(1)} all-gather(bf16[16,128]{1,0:T(8,128)(2,1)S(1)} %fusion.28), channel_id=1, replica_groups=mesh['ctx'=16,'kvh'=8] {'ctx','kvh'}, dimensions={1}, use_global_device_ids=true | all-gather | bytes 528384 | tf_op jit(solution)/shard_map/all_gather | solution.py:85
  270.1 4.8 fusion.38
  274.9 10.5 %fusion.6 = f32[16,16384]{1,0:T(8,128)} fusion(bf16[208,16384]{1,0:T(8,128)(2,1)} %param.19, bf16[16,16384]{1,0:T(8,128)(2,1)S(1)} %all_gather.3, bf16[208,16384]{1,0:T(8,128)(2,1)} %param.18, f32[16,208]{1,0:T(8,128)S(1)} %fusion.38), kind=kOutput, calls=%fused_computation.14 | convolution fusion | flops 218123776 | bytes 15217664 | tf_op jit(solution)/shard_map/dot_general | solution.py:89
  285.4 0.0 reduce-scatter.5.cloned.1.call-update
  285.4 628.9 %reduce-scatter.5.cloned.1.call-done = f32[16,128]{1,0:T(8,128)} async-done(((f32[16,16384]{1,0:T(8,128)}), f32[16,128]{1,0:T(8,128)}) %reduce-scatter.5.cloned.1.call-update) | async-done | bytes 8208 | tf_op jit(solution)/shard_map/reduce_scatter | solution.py:90
  914.3 1.3 fusion.29
  (6 shorter events, 0.0 us)
Async XLA Ops:
  6.5 160.7 %copy-start = (bf16[4,4,128]{2,1,0:T(4,128)(2,1)S(1)}, bf16[4,4,128]{2,1,0:T(4,128)(2,1)}, u32[]{:S(2)}) copy-start(bf16[4,4,128]{2,1,0:T(4,128)(2,1)} %param.14) | copy-start | bytes 12292
  6.5 229.0 %copy-start.1 = (f32[128]{0:T(128)S(1)}, f32[128]{0:T(128)}, u32[]{:S(2)}) copy-start(f32[128]{0:T(128)} %param.16) | copy-start | bytes 1540
  6.5 127.7 %all-reduce.2.cloned.1.call-start = ((), (), s32[]{:S(2)}) async-start(), calls=%async_computation.2 | async-start | bytes 262144 | tf_op jit(solution)/shard_map/psum | solution.py:70
  49.7 117.5 %reduce-scatter.3.cloned.1.call-start = ((), (), s32[]{:S(2)}) async-start(), calls=%async_computation.3 | async-start | bytes 73728 | tf_op jit(solution)/shard_map/reduce_scatter | solution.py:78
  138.7 775.6 %reduce-scatter.5.cloned.1.call-start = ((), (), s32[]{:S(2)}) async-start(), calls=%async_computation.4 | async-start | bytes 1056768 | tf_op jit(solution)/shard_map/reduce_scatter | solution.py:90
Sparse Core Ops, SparseCore 0:
  49.8 84.3 all-reduce.1
  138.8 28.3 reduce-scatter.2
  285.5 628.7 reduce-scatter.4
where the time goes:
time: 929 us; the launch traced here: 922 us
  waiting for transfers between devices  712 us (77%)
  blocking collectives  167 us (18%)
  matrix products  23.4 us (3%)
  between operations  13.2 us (1%)
    reduce_scatter x1, waiting for transfers between devices, per_device(): lax.psum_scatter(down_block, ('ctx', 'kvh'), scatter_dimension=1, tiled=T...  629 us
    psum x1, blocking collectives, per_device(): lax.psum(jnp.sum(carried_wide * carried_wide, axis=1), ('ctx', 'kvh'))  67.5 us
    psum x1, waiting for transfers between devices, per_device(): denominator, numerator = lax.psum((denominator, numerator), 'ctx')  54.9 us
    pmax x1, blocking collectives, per_device(): highest = lax.pmax(local_max, 'ctx')  36.1 us
    all_gather x1, blocking collectives, per_device(): piece = lax.all_gather(normed, ('ctx', 'kvh'), axis=1, tiled=True)  34.5 us
    psum x1, blocking collectives, per_device(): denominator, numerator = lax.psum((denominator, numerator), 'ctx')  29.1 us
    reduce_scatter x1, waiting for transfers between devices, per_device(): lax.psum_scatter(projected_block, 'kvh', scatter_dimension=1, tiled=True)  28.4 us
  transfers between devices with their start and end apart: 3, of which 3 were waited for; matrix products, arithmetic and copies ran while one was open for 0% of the time, Pallas kernels for 0%

commit v1 on v0

v1 whole, which is shorter than its diff:
```python
import functools
import math

import jax
import jax.numpy as jnp
from jax import lax
from jax.experimental import pallas as pl
from jax.experimental.pallas import tpu as pltpu
from jax.sharding import PartitionSpec as P

EPSILON = 1e-05
HIDE = -1e30
LANES = 128
MESH = pl.DeviceIdType.MESH
ROWS_BY_ROWS = (((1,), (1,)), ((), ()))
BF16 = jnp.bfloat16
F32 = jnp.float32


def dot(left, right):
    return jnp.dot(left, right, preferred_element_type=F32)


def dot_rows(left, right):
    return lax.dot_general(left, right, ROWS_BY_ROWS, preferred_element_type=F32)


def drain(ref, sem):
    pltpu.make_async_copy(ref, ref, sem).wait()


def layer_kernel(
    dims,
    query,
    draft,
    lengths,
    residual,
    gain,
    cache_hbm,
    out_hbm,
    gate_hbm,
    up_hbm,
    down_hbm,
    result,
    cache,
    out_w,
    gate_w,
    up_w,
    down_w,
    numer,
    stats,
    att_msg,
    att_in,
    heads,
    proj_msg,
    proj_in,
    gains,
    feats,
    half_wide,
    half_msg,
    half_in,
    pair_msg,
    down_in,
    cache_sem,
    weight_sem,
    send_sem,
    recv_sem,
    feat_sem,
    relay_sem,
    half_sem,
):
    ctx_n, kvh_n, planes, steps, batch = dims
    x_n = kvh_n // 2
    z_n = ctx_n // planes
    per_plane = z_n * x_n
    chips = ctx_n * x_n
    tokens = steps * batch
    shard_len = cache.shape[2]
    scale = 1.0 / math.sqrt(LANES)
    ctx = lax.axis_index("ctx")
    kvh = lax.axis_index("kvh")
    core = lax.rem(kvh, 2)
    chip = ctx * x_n + lax.div(kvh, 2)
    plane = lax.div(ctx, z_n)
    spot = lax.rem(chip, per_plane)
    partner = (ctx, kvh + 1 - 2 * core)

    def chip_device(at):
        return (lax.div(at, x_n), lax.rem(at, x_n) * 2 + core)

    def send(src, dst, at_send, at_recv, device):
        pltpu.make_async_remote_copy(
            src_ref=src,
            dst_ref=dst,
            send_sem=at_send,
            recv_sem=at_recv,
            device_id=device,
            device_id_type=MESH,
        ).start()

    cache_copies = []
    for b in range(batch):
        copy = pltpu.make_async_copy(cache_hbm.at[:, b], cache.at[:, b], cache_sem.at[b])
        copy.start()
        cache_copies.append(copy)
    weight_copies = []
    for at, (src, dst) in enumerate(
        ((out_hbm, out_w), (gate_hbm, gate_w), (up_hbm, up_w), (down_hbm, down_w))
    ):
        copy = pltpu.make_async_copy(src, dst, weight_sem.at[at])
        copy.start()
        weight_copies.append(copy)

    barrier = pltpu.get_barrier_semaphore()

    @pl.loop(1, chips)
    def _(i):
        pl.semaphore_signal(
            barrier, inc=1, device_id=chip_device(lax.rem(chip + i, chips)), device_id_type=MESH
        )

    @pl.loop(0, x_n)
    def _(i):
        pl.semaphore_signal(
            barrier, inc=1, device_id=(ctx, 2 * i + 1 - core), device_id_type=MESH
        )

    lane = lax.broadcasted_iota(jnp.int32, (ctx_n * steps, LANES), 1)
    position = ctx * shard_len + lax.broadcasted_iota(jnp.int32, (ctx_n * steps, shard_len), 1)
    draft_row = lax.broadcasted_iota(jnp.int32, (ctx_n * steps, tokens), 0)
    draft_col = lax.broadcasted_iota(jnp.int32, (ctx_n * steps, tokens), 1)
    draft_step = lax.div(draft_col, batch) + ctx * steps
    for b in range(batch):
        cache_copies[b].wait()
        q = query[b]
        seen = position < lengths[b]
        scores = jnp.where(seen, dot_rows(q, cache[0, b]) * scale, HIDE)
        draft_seen = (draft_step <= lax.rem(draft_row, steps)) & (
            lax.rem(draft_col, batch) == b
        )
        draft_scores = jnp.where(draft_seen, dot_rows(q, draft[0]) * scale, HIDE)
        top = jnp.maximum(
            jnp.max(scores, axis=1, keepdims=True), jnp.max(draft_scores, axis=1, keepdims=True)
        )
        top = top.astype(BF16).astype(F32)
        weights = jnp.where(seen, jnp.exp(scores - top), 0.0)
        draft_weights = jnp.where(draft_seen, jnp.exp(draft_scores - top), 0.0)
        total = jnp.sum(weights, axis=1, keepdims=True) + jnp.sum(
            draft_weights, axis=1, keepdims=True
        )
        values = dot(weights.astype(BF16), cache[1, b]) + dot(draft_weights.astype(BF16), draft[1])
        both = jnp.where(lane < 64, top, total)
        for h in range(ctx_n):
            rows = slice(h * steps, (h + 1) * steps)
            numer[h, b * steps : (b + 1) * steps, :] = values[rows]
            stats[h, b * steps : (b + 1) * steps, :] = both[rows]
    att_msg[:, 0:tokens, :] = numer[...].astype(BF16)
    wide = stats[...]
    high = wide.astype(BF16).astype(F32)
    lanes3 = lax.broadcasted_iota(jnp.int32, wide.shape, 2)
    att_msg[:, tokens : 2 * tokens, :] = jnp.where(lanes3 < 96, high, wide - high).astype(BF16)

    pl.semaphore_wait(barrier, chips - 1 + x_n)

    @pl.loop(1, ctx_n)
    def _(i):
        to = lax.rem(ctx + i, ctx_n)
        send(att_msg.at[to], att_in.at[ctx], send_sem.at[0], recv_sem.at[0], (to, kvh))

    att_in[ctx] = att_msg[ctx]
    gains[kvh, ctx] = gain[...]

    @pl.loop(1, ctx_n)
    def _(i):
        to = lax.rem(ctx + i, ctx_n)
        send(gains.at[kvh, ctx], gains.at[kvh, ctx], send_sem.at[1], recv_sem.at[1], (to, kvh))

    drain(att_in.at[0 : ctx_n - 1], recv_sem.at[0])
    parts = [att_in[i, tokens : 2 * tokens, :].astype(F32) for i in range(ctx_n)]
    tops = [jnp.broadcast_to(p[:, 0:1], (tokens, LANES)) for p in parts]
    highest = functools.reduce(jnp.maximum, tops)
    factors = [jnp.exp(t - highest) for t in tops]
    denominator = sum(f * (p[:, 64:65] + p[:, 96:97]) for f, p in zip(factors, parts))
    numerator = sum(
        f * att_in[i, 0:tokens, :].astype(F32) for i, f in enumerate(factors)
    )
    heads[ctx] = (numerator / denominator).astype(BF16)

    @pl.loop(1, ctx_n)
    def _(i):
        to = lax.rem(ctx + i, ctx_n)
        send(heads.at[ctx], heads.at[ctx], send_sem.at[2], recv_sem.at[2], (to, kvh))

    drain(gains.at[0, 0 : ctx_n - 1], recv_sem.at[1])

    @pl.loop(1, kvh_n)
    def _(i):
        to = lax.rem(kvh + i, kvh_n)
        send(gains.at[kvh], gains.at[kvh], send_sem.at[3], recv_sem.at[3], (ctx, to))

    weight_copies[0].wait()
    drain(heads.at[0 : ctx_n - 1], recv_sem.at[2])
    attended = jnp.concatenate([heads[i] for i in range(ctx_n)], axis=1)
    projected = dot(attended, out_w[...])
    for k in range(kvh_n):
        proj_msg[k] = projected[:, k * LANES : (k + 1) * LANES]

    @pl.loop(1, kvh_n)
    def _(i):
        to = lax.rem(kvh + i, kvh_n)
        send(proj_msg.at[to], proj_in.at[kvh], send_sem.at[4], recv_sem.at[4], (ctx, to))

    proj_in[kvh] = proj_msg[kvh]
    drain(proj_in.at[0 : kvh_n - 1], recv_sem.at[4])
    carried = residual[...].astype(F32)
    for k in range(kvh_n):
        carried = carried + proj_in[k]
    carried = carried.astype(BF16)
    feats[core, chip] = carried

    for d in range(planes):
        first = lax.rem(plane + d, planes) * per_plane

        @pl.loop(1 if d == 0 else 0, per_plane)
        def _(i):
            to = first + lax.rem(spot + i, per_plane)
            send(
                feats.at[core, chip],
                feats.at[core, chip],
                send_sem.at[5],
                feat_sem.at[plane],
                chip_device(to),
            )

    drain(gains.at[0 : kvh_n - 1], recv_sem.at[3])
    weight_copies[1].wait()
    weight_copies[2].wait()
    order = [0] + [d for d in (1, planes - 1, *range(2, planes - 1)) if d < planes]
    order = list(dict.fromkeys(order))
    width = per_plane * 2 * LANES
    gate = jnp.zeros((tokens, gate_w.shape[0]), F32)
    up = jnp.zeros((tokens, gate_w.shape[0]), F32)
    squares = jnp.zeros((tokens, LANES), F32)

    def relay(d):
        at = lax.rem(plane + d, planes)
        first = at * per_plane
        count = per_plane - 1 if d == 0 else per_plane
        drain(feats.at[core, pl.ds(first, count)], feat_sem.at[at])
        block = feats.at[core, pl.ds(first, per_plane)]
        send(block, block, send_sem.at[6], relay_sem.at[at], partner)

    relay(order[0])
    for n, d in enumerate(order):
        if n + 1 < planes:
            relay(order[n + 1])
        at = lax.rem(plane + d, planes)
        first = at * per_plane
        drain(feats.at[1 - core, pl.ds(first, per_plane)], relay_sem.at[at])
        pieces = []
        for s in range(per_plane):
            for c in range(2):
                piece = feats[c, first + s].astype(F32)
                squares = squares + piece * piece
                scaled = piece * gains[s % x_n * 2 + c, at * z_n + s // x_n]
                pieces.append(scaled.astype(BF16))
        rows = jnp.concatenate(pieces, axis=1)
        columns = pl.ds(pl.multiple_of(at * width, width), width)
        gate = gate + dot_rows(rows, gate_w[:, columns])
        up = up + dot_rows(rows, up_w[:, columns])
    mean_square = jnp.sum(squares, axis=1, keepdims=True) / (chips * 2 * LANES)
    inverse = lax.rsqrt(mean_square + EPSILON)
    gate = gate * inverse
    up = up * inverse
    hidden = (gate / (1.0 + jnp.exp(-gate)) * up).astype(BF16)

    weight_copies[3].wait()
    order = order[::-1]

    def halves(n):
        at = lax.rem(plane + order[n], planes)
        columns = pl.ds(pl.multiple_of(at * width, width), width)
        block = dot(hidden, down_w[:, columns])
        for s in range(per_plane):
            for c in range(2):
                piece = block[:, (2 * s + c) * LANES : (2 * s + c + 1) * LANES]
                half_wide[n, c, s] = piece
                half_msg[n, c, s] = piece.astype(BF16)
        send(half_msg.at[n, 1 - core], half_in.at[n], send_sem.at[7], half_sem.at[n], partner)

    def spread(n):
        d = order[n]
        first = lax.rem(plane + d, planes) * per_plane
        drain(half_in.at[n], half_sem.at[n])
        pair_msg[n] = (half_wide[n, core] + half_in[n].astype(F32)).astype(BF16)

        @pl.loop(1 if d == 0 else 0, per_plane)
        def _(i):
            to = lax.rem(spot + i, per_plane)
            send(
                pair_msg.at[n, to],
                down_in.at[chip],
                send_sem.at[8],
                recv_sem.at[5],
                chip_device(first + to),
            )

    for n in range(planes):
        halves(n)
        if n >= 1:
            spread(n - 1)
    spread(planes - 1)
    down_in[chip] = pair_msg[planes - 1, spot]
    drain(down_in.at[0 : chips - 1], recv_sem.at[5])
    final = carried.astype(F32) + jnp.sum(down_in[...].astype(F32), axis=0)
    result[...] = final.astype(BF16)

    drain(att_in.at[0 : ctx_n - 1], send_sem.at[0])
    drain(gains.at[0, 0 : ctx_n - 1], send_sem.at[1])
    drain(heads.at[0 : ctx_n - 1], send_sem.at[2])
    drain(gains.at[0 : kvh_n - 1], send_sem.at[3])
    drain(proj_in.at[0 : kvh_n - 1], send_sem.at[4])
    drain(down_in.at[0 : chips - 1], send_sem.at[5])
    drain(feats.at[0], send_sem.at[6])
    drain(feats.at[0], send_sem.at[7])
    drain(down_in.at[0 : chips - 1], send_sem.at[8])


def per_device(ctx_n, kvh_n, planes, *arguments):
    (
        query,
        new_kv,
        kv_cache,
        lengths,
        residual,
        out_weight,
        norm_gain,
        gate_weight,
        up_weight,
        down_weight,
    ) = arguments
    steps, batch, query_width = query.shape
    heads = query_width // LANES
    assert heads == ctx_n and kv_cache.shape[2] == 1
    tokens = steps * batch
    chips = ctx_n * kvh_n // 2
    per_plane = chips // planes
    queries = query.reshape(steps, batch, heads, LANES).transpose(1, 2, 0, 3)
    queries = queries.reshape(batch, heads * steps, LANES)
    cache = kv_cache.reshape(2, batch, kv_cache.shape[3], LANES)
    vmem = pl.BlockSpec(memory_space=pltpu.VMEM)
    smem = pl.BlockSpec(memory_space=pltpu.SMEM)
    far = pl.BlockSpec(memory_space=pl.ANY)
    dma = pltpu.SemaphoreType.DMA
    out = pl.pallas_call(
        functools.partial(layer_kernel, (ctx_n, kvh_n, planes, steps, batch)),
        out_shape=jax.ShapeDtypeStruct((tokens, LANES), BF16),
        in_specs=[vmem, vmem, smem, vmem, vmem, far, far, far, far, far],
        out_specs=vmem,
        scratch_shapes=[
            pltpu.VMEM(cache.shape, BF16),
            pltpu.VMEM(out_weight.shape, BF16),
            pltpu.VMEM(gate_weight.shape, BF16),
            pltpu.VMEM(up_weight.shape, BF16),
            pltpu.VMEM(down_weight.shape, BF16),
            pltpu.VMEM((ctx_n, tokens, LANES), F32),
            pltpu.VMEM((ctx_n, tokens, LANES), F32),
            pltpu.VMEM((ctx_n, 2 * tokens, LANES), BF16),
            pltpu.VMEM((ctx_n, 2 * tokens, LANES), BF16),
            pltpu.VMEM((ctx_n, tokens, LANES), BF16),
            pltpu.VMEM((kvh_n, tokens, LANES), F32),
            pltpu.VMEM((kvh_n, tokens, LANES), F32),
            pltpu.VMEM((kvh_n, ctx_n, 1, LANES), F32),
            pltpu.VMEM((2, chips, tokens, LANES), BF16),
            pltpu.VMEM((planes, 2, per_plane, tokens, LANES), F32),
            pltpu.VMEM((planes, 2, per_plane, tokens, LANES), BF16),
            pltpu.VMEM((planes, per_plane, tokens, LANES), BF16),
            pltpu.VMEM((planes, per_plane, tokens, LANES), BF16),
            pltpu.VMEM((chips, tokens, LANES), BF16),
            dma((batch,)),
            dma((4,)),
            dma((9,)),
            dma((6,)),
            dma((planes,)),
            dma((planes,)),
            dma((planes,)),
        ],
        compiler_params=pltpu.CompilerParams(
            collective_id=0, has_side_effects=True, vmem_limit_bytes=56 * 2**20
        ),
        name="layer",
    )(
        queries,
        new_kv.reshape(2, tokens, LANES),
        lengths,
        residual.transpose(1, 0, 2).reshape(tokens, LANES),
        norm_gain.reshape(1, LANES),
        cache,
        out_weight,
        gate_weight,
        up_weight,
        down_weight,
    )
    return out.reshape(batch, steps, LANES).transpose(1, 0, 2)


def solution(mesh):
    ctx_n, kvh_n = mesh.shape["ctx"], mesh.shape["kvh"]
    planes = 4 if ctx_n % 4 == 0 and ctx_n > 4 else 2
    return jax.shard_map(
        functools.partial(per_device, ctx_n, kvh_n, planes),
        mesh=mesh,
        in_specs=(
            P(None, None, "kvh"),
            P(None, None, None, "kvh"),
            P(None, None, "kvh", "ctx", None),
            P(),
            P(None, None, ("ctx", "kvh")),
            P("kvh", "ctx"),
            P(("ctx", "kvh")),
            P(("ctx", "kvh"), None),
            P(("ctx", "kvh"), None),
            P(("ctx", "kvh"), None),
        ),
        out_specs=P(None, None, ("ctx", "kvh")),
        check_vma=False,
    )
```

time: 929 us -> 53.7 us (0.06)
  waiting for transfers between devices: 712 us -> 0 us
  blocking collectives: 167 us -> 0 us
  Pallas kernels: 0 us -> 49.4 us
  matrix products: 23.4 us -> 0 us
  between operations: 13.2 us -> 0.01 us
    reduce_scatter x2 -> x0, waiting for transfers between devices: 657 us -> none  [the longest x1 629 us: per_device(): lax.psum_scatter(down_block, ('ctx', 'kvh'), scatter_dimension=1, tiled=T...]
    psum x2 -> x0, blocking collectives: 96.6 us -> none  [the longest x1 67.5 us: per_device(): lax.psum(jnp.sum(carried_wide * carried_wide, axis=1), ('ctx', 'kvh'))]
    psum x1 -> x0, waiting for transfers between devices: 54.9 us -> none  [per_device(): denominator, numerator = lax.psum((denominator, numerator), 'ctx')]
    pallas_call x0 -> x1, Pallas kernels: none -> 49.4 us  [per_device(): pl.pallas_call(functools.partial(layer_kernel, (ctx_n, kvh_n, planes, ste...]
    pmax x1 -> x0, blocking collectives: 36.1 us -> none  [per_device(): highest = lax.pmax(local_max, 'ctx')]
    all_gather x1 -> x0, blocking collectives: 34.5 us -> none  [per_device(): piece = lax.all_gather(normed, ('ctx', 'kvh'), axis=1, tiled=True)]
    dot_general x7 -> x0, matrix products: 23.4 us -> none  [the longest x1 10.5 us: per_device(): jnp.dot(hidden, down_weight, preferred_element_type=jnp.float32)]
  transfers between devices with their start and end apart: 3 -> 0, of which waited for: 3 -> 0; matrix products, arithmetic and copies ran while one was open for 0% -> 0% of each run, Pallas kernels for 0% -> 0%
where the time goes in v1:
time: 53.7 us; the launch traced here: 53.5 us
  Pallas kernels  49.4 us (92%)
  local copies, waits for them, and re-layouts  4.11 us (8%)
    pallas_call x1, Pallas kernels, per_device(): pl.pallas_call(functools.partial(layer_kernel, (ctx_n, kvh_n, planes, ste...  49.4 us
    reshape x2, local copies, waits for them, and re-layouts, per_device(): queries = query.reshape(steps, batch, heads, LANES).transpose(1, 2, 0, 3)  1.56 us
    transpose x1, local copies, waits for them, and re-layouts, per_device(): residual.transpose(1, 0, 2).reshape(tokens, LANES)  1.28 us
    reshape x1, local copies, waits for them, and re-layouts, per_device(): return out.reshape(batch, steps, LANES).transpose(1, 0, 2)  1.27 us

profile of v1, /device:TPU:1, one launch (start us, length us, event | category | flops | bytes accessed | tf_op | source)
XLA Modules:
  0.0 53.5 jit_solution(10683042475109672744)
XLA Ops:
  0.0 0.9 %reshape.21 = bf16[4,4,16,128]{3,2,1,0:T(8,128)(2,1)S(1)} reshape(bf16[4,4,2048]{2,1,0:T(4,128)(2,1)} %param.10) | data formatting | bytes 131072 | tf_op jit(solution)/shard_map/reshape | solution.py:348
  0.9 0.7 %copy.11 = bf16[4,4,16,128]{3,0,2,1:T(4,128)(2,1)} copy(bf16[4,4,16,128]{3,2,1,0:T(8,128)(2,1)S(1)} %reshape.21) | data formatting | bytes 131072 | tf_op jit(solution)/shard_map/reshape | solution.py:348
  1.6 1.3 %copy.12 = bf16[4,4,128]{2,1,0:T(4,128)(2,1)} copy(bf16[4,4,128]{2,0,1:T(4,128)(2,1)} %bitcast.17) | data formatting | bytes 8192 | tf_op jit(solution)/shard_map/transpose | solution.py:396
  2.8 49.4 %layer.1 = bf16[16,128]{1,0:T(8,128)(2,1)} custom-call(bf16[4,64,128]{2,1,0:T(8,128)(2,1)} %bitcast.13, bf16[2,16,128]{2,1,0:T(8,128)(2,1)} %bitcast.16, s32[4]{0:T(128)} %lengths.1, bf16[16,128]{1,0:T(8,128)(2,1)} %bitcast.15, f32[1,128]{1,0:T(1,128)} %bitcast.18, bf16[2,4,1024,128]{3,2,1,0:T(8,128)(2,1)} %bitcast.12, bf16[2048,1024]{1,0:T(8,128)(2,1)} %out_hbm.1, ...), custom_call_target="tpu_custom_call" | custom-call | tf_op jit(solution)/shard_map/layer/pallas_call | solution.py:355
  52.2 1.3 %copy.15 = bf16[4,4,128]{2,0,1:T(4,128)(2,1)} copy(bf16[4,4,128]{2,1,0:T(4,128)(2,1)} %bitcast.14) | data formatting | bytes 8192 | tf_op jit(solution)/shard_map/reshape | solution.py:404

commit v2 on v1

v2 whole, which is shorter than its diff:
```python
import functools
import math

import jax
import jax.numpy as jnp
from jax import lax
from jax.experimental import pallas as pl
from jax.experimental.pallas import tpu as pltpu
from jax.sharding import PartitionSpec as P

EPSILON = 1e-05
HIDE = -1e30
LANES = 128
MESH = pl.DeviceIdType.MESH
ROWS_BY_ROWS = (((1,), (1,)), ((), ()))
BF16 = jnp.bfloat16
F32 = jnp.float32


def dot(left, right):
    return jnp.dot(left, right, preferred_element_type=F32)


def dot_rows(left, right):
    return lax.dot_general(left, right, ROWS_BY_ROWS, preferred_element_type=F32)


def drain(ref, sem):
    pltpu.make_async_copy(ref, ref, sem).wait()


def layer_kernel(
    dims,
    query,
    draft,
    lengths,
    residual,
    gain,
    cache_hbm,
    out_hbm,
    gate_hbm,
    up_hbm,
    down_hbm,
    result,
    cache,
    out_w,
    gate_up_w,
    down_w,
    queries,
    numer,
    stats,
    att_msg,
    att_in,
    heads,
    proj_msg,
    proj_in,
    gains,
    feats,
    half_wide,
    half_msg,
    half_in,
    pair_msg,
    down_in,
    cache_sem,
    weight_sem,
    send_sem,
    recv_sem,
    head_sem,
    feat_sem,
    relay_sem,
    half_sem,
):
    ctx_n, kvh_n, planes, steps, batch = dims
    x_n = kvh_n // 2
    z_n = ctx_n // planes
    chips = ctx_n * x_n
    tokens = steps * batch
    shard_len = cache.shape[2]
    units = down_w.shape[0]
    scale = 1.0 / math.sqrt(LANES)
    ctx = lax.axis_index("ctx")
    kvh = lax.axis_index("kvh")
    core = lax.rem(kvh, 2)
    x = lax.div(kvh, 2)
    chip = ctx * x_n + x
    plane = lax.div(ctx, z_n)
    place = lax.rem(ctx, z_n)
    partner = (ctx, kvh + 1 - 2 * core)

    def far(dy, dz):
        return min(dy, planes - dy) + min(dz, z_n - dz)

    offsets = sorted(
        ((dy, dz) for dy in range(planes) for dz in range(z_n)), key=lambda o: (far(*o), o)
    )
    opposite = [offsets.index((-dy % planes, -dz % z_n)) for dy, dz in offsets]
    hops = [far(*o) for o in offsets]
    class_n = hops[-1] + 1
    bounds = [(hops.index(k), hops.index(k) + hops.count(k)) for k in range(class_n)]
    ctx_at = [
        lax.rem(plane + dy, planes) * z_n + lax.rem(place + dz, z_n) for dy, dz in offsets
    ]

    def send(src, dst, at_send, at_recv, device):
        pltpu.make_async_remote_copy(
            src_ref=src,
            dst_ref=dst,
            send_sem=at_send,
            recv_sem=at_recv,
            device_id=device,
            device_id_type=MESH,
        ).start()

    cache_copies = []
    for b in range(batch):
        copy = pltpu.make_async_copy(cache_hbm.at[:, b], cache.at[:, b], cache_sem.at[b])
        copy.start()
        cache_copies.append(copy)

    barrier = pltpu.get_barrier_semaphore()

    @pl.loop(1, chips)
    def _(i):
        at = lax.rem(chip + i, chips)
        pl.semaphore_signal(
            barrier,
            inc=1,
            device_id=(lax.div(at, x_n), lax.rem(at, x_n) * 2 + core),
            device_id_type=MESH,
        )

    @pl.loop(0, x_n)
    def _(i):
        pl.semaphore_signal(
            barrier, inc=1, device_id=(ctx, 2 * i + 1 - core), device_id_type=MESH
        )

    for t in range(steps):
        row = query[t].astype(F32)
        for h in range(ctx_n):
            at = h * tokens + t * batch
            queries[at : at + batch, :] = row[:, h * LANES : (h + 1) * LANES]

    lane = lax.broadcasted_iota(jnp.int32, (ctx_n * steps, LANES), 1)
    position = ctx * shard_len + lax.broadcasted_iota(jnp.int32, (ctx_n * steps, shard_len), 1)
    draft_row = lax.broadcasted_iota(jnp.int32, (ctx_n * steps, tokens), 0)
    draft_col = lax.broadcasted_iota(jnp.int32, (ctx_n * steps, tokens), 1)
    draft_step = lax.div(draft_col, batch) + ctx * steps
    weight_copies = []
    for b in range(batch):
        cache_copies[b].wait()
        if b == batch - 1:
            for at, (src, dst) in enumerate(
                (
                    (out_hbm, out_w),
                    (gate_hbm, gate_up_w.at[0:units]),
                    (up_hbm, gate_up_w.at[units : 2 * units]),
                    (down_hbm, down_w),
                )
            ):
                copy = pltpu.make_async_copy(src, dst, weight_sem.at[at])
                copy.start()
                weight_copies.append(copy)
        mine = pl.ds(b, ctx_n * steps, stride=batch)
        q = queries[mine, :].astype(BF16)
        seen = position < lengths[b]
        scores = jnp.where(seen, dot_rows(q, cache[0, b]) * scale, HIDE)
        draft_seen = (draft_step <= lax.rem(draft_row, steps)) & (
            lax.rem(draft_col, batch) == b
        )
        draft_scores = jnp.where(draft_seen, dot_rows(q, draft[0]) * scale, HIDE)
        top = jnp.maximum(
            jnp.max(scores, axis=1, keepdims=True), jnp.max(draft_scores, axis=1, keepdims=True)
        )
        top = top.astype(BF16).astype(F32)
        weights = jnp.where(seen, jnp.exp(scores - top), 0.0)
        draft_weights = jnp.where(draft_seen, jnp.exp(draft_scores - top), 0.0)
        total = jnp.sum(weights, axis=1, keepdims=True) + jnp.sum(
            draft_weights, axis=1, keepdims=True
        )
        numer[mine, :] = dot(weights.astype(BF16), cache[1, b]) + dot(
            draft_weights.astype(BF16), draft[1]
        )
        stats[mine, :] = jnp.where(lane < 64, top, total)
    by_head = (ctx_n, tokens, LANES)
    att_msg[:, 0:tokens, :] = numer[...].reshape(by_head).astype(BF16)
    wide = stats[...].reshape(by_head)
    high = wide.astype(BF16).astype(F32)
    lanes3 = lax.broadcasted_iota(jnp.int32, by_head, 2)
    att_msg[:, tokens : 2 * tokens, :] = jnp.where(lanes3 < 96, high, wide - high).astype(BF16)

    pl.semaphore_wait(barrier, chips - 1 + x_n)

    for n in range(1, ctx_n):
        to = ctx_at[n]
        send(att_msg.at[to], att_in.at[opposite[n]], send_sem.at[0], recv_sem.at[0], (to, kvh))
    att_in[0] = att_msg[ctx]
    gains[kvh, ctx] = gain[...]

    @pl.loop(1, ctx_n)
    def _(i):
        to = lax.rem(ctx + i, ctx_n)
        send(gains.at[kvh, ctx], gains.at[kvh, ctx], send_sem.at[1], recv_sem.at[1], (to, kvh))

    drain(att_in.at[0 : ctx_n - 1], recv_sem.at[0])
    parts = [att_in[i, tokens : 2 * tokens, :].astype(F32) for i in range(ctx_n)]
    tops = [jnp.broadcast_to(p[:, 0:1], (tokens, LANES)) for p in parts]
    highest = functools.reduce(jnp.maximum, tops)
    factors = [jnp.exp(t - highest) for t in tops]
    denominator = sum(f * (p[:, 64:65] + p[:, 96:97]) for f, p in zip(factors, parts))
    numerator = sum(
        f * att_in[i, 0:tokens, :].astype(F32) for i, f in enumerate(factors)
    )
    heads[0] = (numerator / denominator).astype(BF16)

    for n in range(1, ctx_n):
        send(
            heads.at[0],
            heads.at[opposite[n]],
            send_sem.at[2],
            head_sem.at[hops[n]],
            (ctx_at[n], kvh),
        )

    drain(gains.at[0, 0 : ctx_n - 1], recv_sem.at[1])

    @pl.loop(1, kvh_n)
    def _(i):
        to = lax.rem(kvh + i, kvh_n)
        send(gains.at[kvh], gains.at[kvh], send_sem.at[3], recv_sem.at[3], (ctx, to))

    weight_copies[0].wait()
    projected = jnp.zeros((tokens, kvh_n * LANES), F32)
    for group in ([0, 1], [2], list(range(3, class_n))):
        group = [k for k in group if k < class_n]
        if not group:
            continue
        low, high = bounds[group[0]][0], bounds[group[-1]][1]
        for k in group:
            if k > 0:
                drain(heads.at[bounds[k][0] : bounds[k][1]], head_sem.at[k])
        attended = jnp.concatenate([heads[n] for n in range(low, high)], axis=1)
        rows = jnp.concatenate(
            [
                out_w[pl.ds(pl.multiple_of(ctx_at[n] * LANES, LANES), LANES), :]
                for n in range(low, high)
            ],
            axis=0,
        )
        projected = projected + dot(attended, rows)
    for k in range(kvh_n):
        proj_msg[k] = projected[:, k * LANES : (k + 1) * LANES]

    @pl.loop(1, kvh_n)
    def _(i):
        to = lax.rem(kvh + i, kvh_n)
        send(proj_msg.at[to], proj_in.at[kvh], send_sem.at[4], recv_sem.at[4], (ctx, to))

    proj_in[kvh] = proj_msg[kvh]
    drain(gains.at[0 : kvh_n - 1], recv_sem.at[3])
    drain(proj_in.at[0 : kvh_n - 1], recv_sem.at[4])
    carried = residual[...].astype(F32)
    for k in range(kvh_n):
        carried = carried + proj_in[k]
    carried = carried.astype(BF16)
    feats[core, 0, x] = carried

    for n in range(ctx_n):

        @pl.loop(1 if n == 0 else 0, x_n)
        def _(i):
            send(
                feats.at[core, 0, x],
                feats.at[core, opposite[n], x],
                send_sem.at[5],
                feat_sem.at[hops[n]],
                (ctx_at[n], lax.rem(x + i, x_n) * 2 + core),
            )

    width = kvh_n * LANES
    products = jnp.zeros((tokens, 2 * units), F32)
    squares = jnp.zeros((tokens, LANES), F32)

    def relay(k):
        low, high = bounds[k]
        drain(feats.at[core, 0, 0 : x_n - 1] if k == 0 else feats.at[core, low:high], feat_sem.at[k])
        block = feats.at[core, low:high]
        send(block, block, send_sem.at[6], relay_sem.at[k], partner)

    weight_copies[1].wait()
    weight_copies[2].wait()
    relay(0)
    for k in range(class_n):
        if k + 1 < class_n:
            relay(k + 1)
        low, high = bounds[k]
        drain(feats.at[1 - core, low:high], relay_sem.at[k])
        for n in range(low, high):
            pieces = []
            for j in range(kvh_n):
                piece = feats[j % 2, n, j // 2].astype(F32)
                squares = squares + piece * piece
                pieces.append((piece * gains[j, ctx_at[n]]).astype(BF16))
            rows = jnp.concatenate(pieces, axis=1)
            columns = pl.ds(pl.multiple_of(ctx_at[n] * width, width), width)
            products = products + dot_rows(rows, gate_up_w[:, columns])
    mean_square = jnp.sum(squares, axis=1, keepdims=True) / (chips * 2 * LANES)
    products = products * lax.rsqrt(mean_square + EPSILON)
    gate = products[:, 0:units]
    up = products[:, units : 2 * units]
    hidden = (gate / (1.0 + jnp.exp(-gate)) * up).astype(BF16)

    weight_copies[3].wait()
    groups = [bounds[k] for k in range(class_n - 1, 1, -1)] + [(0, bounds[1][1])]

    def halves(g):
        low, high = groups[g]
        for n in range(low, high):
            columns = pl.ds(pl.multiple_of(ctx_at[n] * width, width), width)
            block = dot(hidden, down_w[:, columns])
            for j in range(kvh_n):
                piece = block[:, j * LANES : (j + 1) * LANES]
                half_wide[j % 2, n, j // 2] = piece
                half_msg[j % 2, n, j // 2] = piece.astype(BF16)
        send(
            half_msg.at[1 - core, low:high],
            half_in.at[low:high],
            send_sem.at[7],
            half_sem.at[g],
            partner,
        )

    def spread(g):
        low, high = groups[g]
        drain(half_in.at[low:high], half_sem.at[g])
        pair_msg[low:high] = (half_wide[core, low:high] + half_in[low:high].astype(F32)).astype(
            BF16
        )
        for n in range(low, high):

            @pl.loop(1 if n == 0 else 0, x_n)
            def _(i):
                to = lax.rem(x + i, x_n)
                send(
                    pair_msg.at[n, to],
                    down_in.at[chip],
                    send_sem.at[8],
                    recv_sem.at[5],
                    (ctx_at[n], to * 2 + core),
                )

    for g in range(len(groups)):
        halves(g)
        if g >= 1:
            spread(g - 1)
    spread(len(groups) - 1)
    down_in[chip] = pair_msg[0, x]
    drain(down_in.at[0 : chips - 1], recv_sem.at[5])
    final = carried.astype(F32) + jnp.sum(down_in[...].astype(F32), axis=0)
    result[...] = final.astype(BF16)

    drain(att_in.at[0 : ctx_n - 1], send_sem.at[0])
    drain(gains.at[0, 0 : ctx_n - 1], send_sem.at[1])
    drain(heads.at[0 : ctx_n - 1], send_sem.at[2])
    drain(gains.at[0 : kvh_n - 1], send_sem.at[3])
    drain(proj_in.at[0 : kvh_n - 1], send_sem.at[4])
    drain(down_in.at[0 : chips - 1], send_sem.at[5])
    drain(feats.at[0], send_sem.at[6])
    drain(half_in, send_sem.at[7])
    drain(down_in.at[0 : chips - 1], send_sem.at[8])


def per_device(ctx_n, kvh_n, planes, *arguments):
    (
        query,
        new_kv,
        kv_cache,
        lengths,
        residual,
        out_weight,
        norm_gain,
        gate_weight,
        up_weight,
        down_weight,
    ) = arguments
    steps, batch, query_width = query.shape
    heads = query_width // LANES
    assert heads == ctx_n and kv_cache.shape[2] == 1
    tokens = steps * batch
    chips = ctx_n * kvh_n // 2
    x_n = kvh_n // 2
    classes = planes // 2 + ctx_n // planes // 2 + 1
    cache = kv_cache.reshape(2, batch, kv_cache.shape[3], LANES)
    units = gate_weight.shape[0]
    vmem = pl.BlockSpec(memory_space=pltpu.VMEM)
    smem = pl.BlockSpec(memory_space=pltpu.SMEM)
    far = pl.BlockSpec(memory_space=pl.ANY)
    dma = pltpu.SemaphoreType.DMA
    out = pl.pallas_call(
        functools.partial(layer_kernel, (ctx_n, kvh_n, planes, steps, batch)),
        out_shape=jax.ShapeDtypeStruct((tokens, LANES), BF16),
        in_specs=[vmem, vmem, smem, vmem, vmem, far, far, far, far, far],
        out_specs=vmem,
        scratch_shapes=[
            pltpu.VMEM(cache.shape, BF16),
            pltpu.VMEM(out_weight.shape, BF16),
            pltpu.VMEM((2 * units, gate_weight.shape[1]), BF16),
            pltpu.VMEM(down_weight.shape, BF16),
            pltpu.VMEM((ctx_n * tokens, LANES), F32),
            pltpu.VMEM((ctx_n * tokens, LANES), F32),
            pltpu.VMEM((ctx_n * tokens, LANES), F32),
            pltpu.VMEM((ctx_n, 2 * tokens, LANES), BF16),
            pltpu.VMEM((ctx_n, 2 * tokens, LANES), BF16),
            pltpu.VMEM((ctx_n, tokens, LANES), BF16),
            pltpu.VMEM((kvh_n, tokens, LANES), F32),
            pltpu.VMEM((kvh_n, tokens, LANES), F32),
            pltpu.VMEM((kvh_n, ctx_n, 1, LANES), F32),
            pltpu.VMEM((2, ctx_n, x_n, tokens, LANES), BF16),
            pltpu.VMEM((2, ctx_n, x_n, tokens, LANES), F32),
            pltpu.VMEM((2, ctx_n, x_n, tokens, LANES), BF16),
            pltpu.VMEM((ctx_n, x_n, tokens, LANES), BF16),
            pltpu.VMEM((ctx_n, x_n, tokens, LANES), BF16),
            pltpu.VMEM((chips, tokens, LANES), BF16),
            dma((batch,)),
            dma((4,)),
            dma((9,)),
            dma((6,)),
            dma((classes,)),
            dma((classes,)),
            dma((classes,)),
            dma((classes,)),
        ],
        compiler_params=pltpu.CompilerParams(
            collective_id=0, has_side_effects=True, vmem_limit_bytes=56 * 2**20
        ),
        name="layer",
    )(
        query,
        new_kv.reshape(2, tokens, LANES),
        lengths,
        residual.reshape(tokens, LANES),
        norm_gain.reshape(1, LANES),
        cache,
        out_weight,
        gate_weight,
        up_weight,
        down_weight,
    )
    return out.reshape(steps, batch, LANES)


def solution(mesh):
    ctx_n, kvh_n = mesh.shape["ctx"], mesh.shape["kvh"]
    planes = 4 if ctx_n % 4 == 0 and ctx_n > 4 else 2
    return jax.shard_map(
        functools.partial(per_device, ctx_n, kvh_n, planes),
        mesh=mesh,
        in_specs=(
            P(None, None, "kvh"),
            P(None, None, None, "kvh"),
            P(None, None, "kvh", "ctx", None),
            P(),
            P(None, None, ("ctx", "kvh")),
            P("kvh", "ctx"),
            P(("ctx", "kvh")),
            P(("ctx", "kvh"), None),
            P(("ctx", "kvh"), None),
            P(("ctx", "kvh"), None),
        ),
        out_specs=P(None, None, ("ctx", "kvh")),
        check_vma=False,
    )
```

time: 53.7 us -> 47.3 us (0.88)
  Pallas kernels: 49.4 us -> 45.8 us
  local copies, waits for them, and re-layouts: 4.11 us -> 1.28 us
    pallas_call x1, Pallas kernels: 49.4 us -> 45.8 us  [per_device(): pl.pallas_call(functools.partial(layer_kernel, (ctx_n, kvh_n, planes, ste...]
    reshape x3 -> x0, local copies, waits for them, and re-layouts: 2.83 us -> none  [the longest x2 1.56 us: per_device(): queries = query.reshape(steps, batch, heads, LANES).transpose(1, 2, 0, 3)]
    transpose x1 -> x0, local copies, waits for them, and re-layouts: 1.28 us -> none  [per_device(): residual.transpose(1, 0, 2).reshape(tokens, LANES)]
    unnamed x0 -> x1, local copies, waits for them, and re-layouts: none -> 1.28 us
where the time goes in v2:
time: 47.3 us; the launch traced here: 47.1 us
  Pallas kernels  45.8 us (97%)
  local copies, waits for them, and re-layouts  1.28 us (3%)
    pallas_call x1, Pallas kernels, per_device(): pl.pallas_call(functools.partial(layer_kernel, (ctx_n, kvh_n, planes, ste...  45.8 us
    unnamed x1, local copies, waits for them, and re-layouts  1.28 us

profile of v2, /device:TPU:1, one launch (start us, length us, event | category | flops | bytes accessed | tf_op | source)
XLA Modules:
  0.0 47.1 jit_solution(16888433468664257230)
XLA Ops:
  0.0 45.8 %layer.1 = bf16[16,128]{1,0:T(8,128)(2,1)} custom-call(bf16[4,4,2048]{2,1,0:T(4,128)(2,1)} %query.1, bf16[2,16,128]{2,1,0:T(8,128)(2,1)} %bitcast.7, s32[4]{0:T(128)} %lengths.1, bf16[16,128]{1,0:T(8,128)(2,1)} %bitcast.8, f32[1,128]{1,0:T(1,128)} %bitcast.9, bf16[2,4,1024,128]{3,2,1,0:T(8,128)(2,1)} %bitcast.5, bf16[2048,1024]{1,0:T(8,128)(2,1)} %out_hbm.1, ...), custom_call_target="tpu_custom_call" | custom-call | tf_op jit(solution)/shard_map/layer/pallas_call | solution.py:399
  45.9 1.3 %copy.12 = bf16[4,4,128]{2,1,0:T(4,128)(2,1)} copy(bf16[4,4,128]{2,1,0:T(4,128)(2,1)} %bitcast.6) | data formatting | bytes 8192

commit v3 on v2

--- a/solution.py
+++ b/solution.py
@@ -1,4 +1,5 @@
 import functools
+import itertools
 import math
 
 import jax
@@ -29,19 +30,29 @@
     pltpu.make_async_copy(ref, ref, sem).wait()
 
 
+def chip_groups(*sizes):
+    longest = sum(size // 2 for size in sizes)
+    return [(0, 1), *((k, k) for k in range(2, longest - 1)), (longest - 1, longest)]
+
+
 def layer_kernel(
     dims,
-    query,
-    draft,
-    lengths,
-    residual,
-    gain,
+    query_hbm,
+    draft_hbm,
+    lengths_hbm,
+    residual_hbm,
+    gain_hbm,
     cache_hbm,
     out_hbm,
     gate_hbm,
     up_hbm,
     down_hbm,
     result,
+    query,
+    draft,
+    lengths,
+    residual,
+    gain,
     cache,
     out_w,
     gate_up_w,
@@ -61,10 +72,12 @@
     half_in,
     pair_msg,
     down_in,
+    input_sem,
     cache_sem,
     weight_sem,
     send_sem,
     recv_sem,
+    part_sem,
     head_sem,
     feat_sem,
     relay_sem,
@@ -87,19 +100,32 @@
     place = lax.rem(ctx, z_n)
     partner = (ctx, kvh + 1 - 2 * core)
 
-    def far(dy, dz):
-        return min(dy, planes - dy) + min(dz, z_n - dz)
-
-    offsets = sorted(
-        ((dy, dz) for dy in range(planes) for dz in range(z_n)), key=lambda o: (far(*o), o)
-    )
-    opposite = [offsets.index((-dy % planes, -dz % z_n)) for dy, dz in offsets]
-    hops = [far(*o) for o in offsets]
-    class_n = hops[-1] + 1
-    bounds = [(hops.index(k), hops.index(k) + hops.count(k)) for k in range(class_n)]
-    ctx_at = [
-        lax.rem(plane + dy, planes) * z_n + lax.rem(place + dz, z_n) for dy, dz in offsets
-    ]
+    def ring(at, size):
+        return min(at, size - at)
+
+    def ordered(*sizes):
+        at = itertools.product(*(range(size) for size in sizes))
+        hops = lambda o: sum(ring(a, size) for a, size in zip(o, sizes))
+        offsets = sorted(at, key=lambda o: (hops(o), o))
+        opposite = [
+            offsets.index(tuple(-a % size for a, size in zip(o, sizes))) for o in offsets
+        ]
+        return offsets, opposite, [hops(o) for o in offsets]
+
+    def ctx_of(dy, dz):
+        return lax.rem(plane + dy, planes) * z_n + lax.rem(place + dz, z_n)
+
+    def span(hops, low, high):
+        inside = [n for n, h in enumerate(hops) if low <= h <= high]
+        return inside[0], inside[-1] + 1
+
+    offsets, opposite, hops = ordered(planes, z_n)
+    ctx_at = [ctx_of(*o) for o in offsets]
+    chip_offsets, chip_opposite, chip_hops = ordered(planes, z_n, x_n)
+    chip_at = [(ctx_of(dy, dz), lax.rem(x + dx, x_n)) for dy, dz, dx in chip_offsets]
+    cuts = chip_groups(planes, z_n, x_n)
+    groups = [span(chip_hops, low, high) for low, high in cuts]
+    group_at = [[low <= h <= high for low, high in cuts].index(True) for h in chip_hops]
 
     def send(src, dst, at_send, at_recv, device):
         pltpu.make_async_remote_copy(
@@ -111,6 +137,19 @@
             device_id_type=MESH,
         ).start()
 
+    inputs = []
+    for at, (src, dst) in enumerate(
+        (
+            (query_hbm, query),
+            (draft_hbm, draft),
+            (lengths_hbm, lengths),
+            (residual_hbm, residual),
+            (gain_hbm, gain),
+        )
+    ):
+        copy = pltpu.make_async_copy(src, dst, input_sem.at[at])
+        copy.start()
+        inputs.append(copy)
     cache_copies = []
     for b in range(batch):
         copy = pltpu.make_async_copy(cache_hbm.at[:, b], cache.at[:, b], cache_sem.at[b])
@@ -119,21 +158,20 @@
 
     barrier = pltpu.get_barrier_semaphore()
 
-    @pl.loop(1, chips)
-    def _(i):
-        at = lax.rem(chip + i, chips)
-        pl.semaphore_signal(
-            barrier,
-            inc=1,
-            device_id=(lax.div(at, x_n), lax.rem(at, x_n) * 2 + core),
-            device_id_type=MESH,
-        )
-
-    @pl.loop(0, x_n)
+    @pl.loop(1, ctx_n)
     def _(i):
         pl.semaphore_signal(
-            barrier, inc=1, device_id=(ctx, 2 * i + 1 - core), device_id_type=MESH
-        )
+            barrier, inc=1, device_id=(lax.rem(ctx + i, ctx_n), kvh), device_id_type=MESH
+        )
+
+    @pl.loop(1, kvh_n)
+    def _(i):
+        pl.semaphore_signal(
+            barrier, inc=1, device_id=(ctx, lax.rem(kvh + i, kvh_n)), device_id_type=MESH
+        )
+
+    for copy in inputs:
+        copy.wait()
 
     for t in range(steps):
         row = query[t].astype(F32)
@@ -189,11 +227,17 @@
     lanes3 = lax.broadcasted_iota(jnp.int32, by_head, 2)
     att_msg[:, tokens : 2 * tokens, :] = jnp.where(lanes3 < 96, high, wide - high).astype(BF16)
 
-    pl.semaphore_wait(barrier, chips - 1 + x_n)
+    pl.semaphore_wait(barrier, ctx_n + kvh_n - 2)
 
     for n in range(1, ctx_n):
         to = ctx_at[n]
-        send(att_msg.at[to], att_in.at[opposite[n]], send_sem.at[0], recv_sem.at[0], (to, kvh))
+        send(
+            att_msg.at[to],
+            att_in.at[opposite[n]],
+            send_sem.at[0],
+            part_sem.at[0 if hops[n] <= 2 else 1],
+            (to, kvh),
+        )
     att_in[0] = att_msg[ctx]
     gains[kvh, ctx] = gain[...]
 
@@ -202,15 +246,27 @@
         to = lax.rem(ctx + i, ctx_n)
         send(gains.at[kvh, ctx], gains.at[kvh, ctx], send_sem.at[1], recv_sem.at[1], (to, kvh))
 
-    drain(att_in.at[0 : ctx_n - 1], recv_sem.at[0])
-    parts = [att_in[i, tokens : 2 * tokens, :].astype(F32) for i in range(ctx_n)]
-    tops = [jnp.broadcast_to(p[:, 0:1], (tokens, LANES)) for p in parts]
-    highest = functools.reduce(jnp.maximum, tops)
-    factors = [jnp.exp(t - highest) for t in tops]
-    denominator = sum(f * (p[:, 64:65] + p[:, 96:97]) for f, p in zip(factors, parts))
-    numerator = sum(
-        f * att_in[i, 0:tokens, :].astype(F32) for i, f in enumerate(factors)
-    )
+    def merged(low, high):
+        parts = [att_in[i, tokens : 2 * tokens, :].astype(F32) for i in range(low, high)]
+        tops = [jnp.broadcast_to(p[:, 0:1], (tokens, LANES)) for p in parts]
+        highest = functools.reduce(jnp.maximum, tops)
+        factors = [jnp.exp(t - highest) for t in tops]
+        denominator = sum(f * (p[:, 64:65] + p[:, 96:97]) for f, p in zip(factors, parts))
+        numerator = sum(
+            f * att_in[low + i, 0:tokens, :].astype(F32) for i, f in enumerate(factors)
+        )
+        return highest, denominator, numerator
+
+    low, high = span(hops, 0, 2)
+    drain(att_in.at[0 : high - 1], part_sem.at[0])
+    highest, denominator, numerator = merged(low, high)
+    if high < ctx_n:
+        drain(att_in.at[high:ctx_n], part_sem.at[1])
+        highest2, denominator2, numerator2 = merged(high, ctx_n)
+        top = jnp.maximum(highest, highest2)
+        factor, factor2 = jnp.exp(highest - top), jnp.exp(highest2 - top)
+        denominator = factor * denominator + factor2 * denominator2
+        numerator = factor * numerator + factor2 * numerator2
     heads[0] = (numerator / denominator).astype(BF16)
 
     for n in range(1, ctx_n):
@@ -218,7 +274,7 @@
             heads.at[0],
             heads.at[opposite[n]],
             send_sem.at[2],
-            head_sem.at[hops[n]],
+            head_sem.at[max(hops[n] - 1, 0)],
             (ctx_at[n], kvh),
         )
 
@@ -231,14 +287,13 @@
 
     weight_copies[0].wait()
     projected = jnp.zeros((tokens, kvh_n * LANES), F32)
-    for group in ([0, 1], [2], list(range(3, class_n))):
-        group = [k for k in group if k < class_n]
-        if not group:
+    for at, (first, last) in enumerate(((0, 1), (2, 2), (3, hops[-1]))):
+        if first > last:
             continue
-        low, high = bounds[group[0]][0], bounds[group[-1]][1]
-        for k in group:
-            if k > 0:
-                drain(heads.at[bounds[k][0] : bounds[k][1]], head_sem.at[k])
+        low, high = span(hops, first, last)
+        for k in range(max(first, 1), last + 1):
+            start, end = span(hops, k, k)
+            drain(heads.at[start:end], head_sem.at[k - 1])
         attended = jnp.concatenate([heads[n] for n in range(low, high)], axis=1)
         rows = jnp.concatenate(
             [
@@ -249,7 +304,7 @@
         )
         projected = projected + dot(attended, rows)
     for k in range(kvh_n):
-        proj_msg[k] = projected[:, k * LANES : (k + 1) * LANES]
+        proj_msg[k] = projected[:, k * LANES : (k + 1) * LANES].astype(BF16)
 
     @pl.loop(1, kvh_n)
     def _(i):
@@ -261,49 +316,55 @@
     drain(proj_in.at[0 : kvh_n - 1], recv_sem.at[4])
     carried = residual[...].astype(F32)
     for k in range(kvh_n):
-        carried = carried + proj_in[k]
+        carried = carried + proj_in[k].astype(F32)
     carried = carried.astype(BF16)
-    feats[core, 0, x] = carried
-
-    for n in range(ctx_n):
-
-        @pl.loop(1 if n == 0 else 0, x_n)
-        def _(i):
-            send(
-                feats.at[core, 0, x],
-                feats.at[core, opposite[n], x],
-                send_sem.at[5],
-                feat_sem.at[hops[n]],
-                (ctx_at[n], lax.rem(x + i, x_n) * 2 + core),
-            )
-
-    width = kvh_n * LANES
+    feats[core, 0] = carried
+
+    far_hops = cuts[-1][0]
+    outward = sorted(range(1, chips), key=lambda n: (chip_hops[n] < far_hops, n))
+    for n in outward:
+        to_ctx, to_x = chip_at[n]
+        send(
+            feats.at[core, 0],
+            feats.at[core, chip_opposite[n]],
+            send_sem.at[5],
+            feat_sem.at[group_at[n]],
+            (to_ctx, to_x * 2 + core),
+        )
+
+    width = 2 * LANES
     products = jnp.zeros((tokens, 2 * units), F32)
     squares = jnp.zeros((tokens, LANES), F32)
 
-    def relay(k):
-        low, high = bounds[k]
-        drain(feats.at[core, 0, 0 : x_n - 1] if k == 0 else feats.at[core, low:high], feat_sem.at[k])
+    def chip_columns(n):
+        at_ctx, at_x = chip_at[n]
+        return pl.ds(pl.multiple_of((at_ctx * x_n + at_x) * width, width), width)
+
+    def relay(g):
+        low, high = groups[g]
+        drain(feats.at[core, low : high - 1 if g == 0 else high], feat_sem.at[g])
         block = feats.at[core, low:high]
-        send(block, block, send_sem.at[6], relay_sem.at[k], partner)
+        send(block, block, send_sem.at[6], relay_sem.at[g], partner)
 
     weight_copies[1].wait()
     weight_copies[2].wait()
     relay(0)
-    for k in range(class_n):
-        if k + 1 < class_n:
-            relay(k + 1)
-        low, high = bounds[k]
-        drain(feats.at[1 - core, low:high], relay_sem.at[k])
+    for g, (low, high) in enumerate(groups):
+        if g + 1 < len(groups):
+            relay(g + 1)
+        drain(feats.at[1 - core, low:high], relay_sem.at[g])
+        pieces = []
         for n in range(low, high):
-            pieces = []
-            for j in range(kvh_n):
-                piece = feats[j % 2, n, j // 2].astype(F32)
+            at_ctx, at_x = chip_at[n]
+            for c in range(2):
+                piece = feats[c, n].astype(F32)
                 squares = squares + piece * piece
-                pieces.append((piece * gains[j, ctx_at[n]]).astype(BF16))
-            rows = jnp.concatenate(pieces, axis=1)
-            columns = pl.ds(pl.multiple_of(ctx_at[n] * width, width), width)
-            products = products + dot_rows(rows, gate_up_w[:, columns])
+                pieces.append((piece * gains[at_x * 2 + c, at_ctx]).astype(BF16))
+        rows = jnp.concatenate(pieces, axis=1)
+        matching = jnp.concatenate(
+            [gate_up_w[:, chip_columns(n)] for n in range(low, high)], axis=1
+        )
+        products = products + dot_rows(rows, matching)
     mean_square = jnp.sum(squares, axis=1, keepdims=True) / (chips * 2 * LANES)
     products = products * lax.rsqrt(mean_square + EPSILON)
     gate = products[:, 0:units]
@@ -311,17 +372,18 @@
     hidden = (gate / (1.0 + jnp.exp(-gate)) * up).astype(BF16)
 
     weight_copies[3].wait()
-    groups = [bounds[k] for k in range(class_n - 1, 1, -1)] + [(0, bounds[1][1])]
+    groups = groups[:1:-1] + [(0, groups[1][1])]
 
     def halves(g):
         low, high = groups[g]
+        matching = jnp.concatenate([down_w[:, chip_columns(n)] for n in range(low, high)], axis=1)
+        block = dot(hidden, matching)
         for n in range(low, high):
-            columns = pl.ds(pl.multiple_of(ctx_at[n] * width, width), width)
-            block = dot(hidden, down_w[:, columns])
-            for j in range(kvh_n):
-                piece = block[:, j * LANES : (j + 1) * LANES]
-                half_wide[j % 2, n, j // 2] = piece
-                half_msg[j % 2, n, j // 2] = piece.astype(BF16)
+            for c in range(2):
+                at = (n - low) * width + c * LANES
+                piece = block[:, at : at + LANES]
+                half_wide[c, n] = piece
+                half_msg[c, n] = piece.astype(BF16)
         send(
             half_msg.at[1 - core, low:high],
             half_in.at[low:high],
@@ -336,25 +398,22 @@
         pair_msg[low:high] = (half_wide[core, low:high] + half_in[low:high].astype(F32)).astype(
             BF16
         )
-        for n in range(low, high):
-
-            @pl.loop(1 if n == 0 else 0, x_n)
-            def _(i):
-                to = lax.rem(x + i, x_n)
-                send(
-                    pair_msg.at[n, to],
-                    down_in.at[chip],
-                    send_sem.at[8],
-                    recv_sem.at[5],
-                    (ctx_at[n], to * 2 + core),
-                )
+        for n in range(high - 1, max(low, 1) - 1, -1):
+            to_ctx, to_x = chip_at[n]
+            send(
+                pair_msg.at[n],
+                down_in.at[chip_opposite[n]],
+                send_sem.at[8],
+                recv_sem.at[5],
+                (to_ctx, to_x * 2 + core),
+            )
 
     for g in range(len(groups)):
         halves(g)
         if g >= 1:
             spread(g - 1)
     spread(len(groups) - 1)
-    down_in[chip] = pair_msg[0, x]
+    down_in[0] = pair_msg[0]
     drain(down_in.at[0 : chips - 1], recv_sem.at[5])
     final = carried.astype(F32) + jnp.sum(down_in[...].astype(F32), axis=0)
     result[...] = final.astype(BF16)
@@ -389,19 +448,23 @@
     tokens = steps * batch
     chips = ctx_n * kvh_n // 2
     x_n = kvh_n // 2
-    classes = planes // 2 + ctx_n // planes // 2 + 1
+    group_n = len(chip_groups(planes, ctx_n // planes, x_n))
     cache = kv_cache.reshape(2, batch, kv_cache.shape[3], LANES)
     units = gate_weight.shape[0]
     vmem = pl.BlockSpec(memory_space=pltpu.VMEM)
-    smem = pl.BlockSpec(memory_space=pltpu.SMEM)
     far = pl.BlockSpec(memory_space=pl.ANY)
     dma = pltpu.SemaphoreType.DMA
     out = pl.pallas_call(
         functools.partial(layer_kernel, (ctx_n, kvh_n, planes, steps, batch)),
-        out_shape=jax.ShapeDtypeStruct((tokens, LANES), BF16),
-        in_specs=[vmem, vmem, smem, vmem, vmem, far, far, far, far, far],
+        out_shape=pltpu.VMEM((tokens, LANES), BF16),
+        in_specs=[far] * 10,
         out_specs=vmem,
         scratch_shapes=[
+            pltpu.VMEM(query.shape, BF16),
+            pltpu.VMEM((2, tokens, LANES), BF16),
+            pltpu.SMEM((batch,), jnp.int32),
+            pltpu.VMEM((tokens, LANES), BF16),
+            pltpu.VMEM((1, LANES), F32),
             pltpu.VMEM(cache.shape, BF16),
             pltpu.VMEM(out_weight.shape, BF16),
             pltpu.VMEM((2 * units, gate_weight.shape[1]), BF16),
@@ -412,23 +475,25 @@
             pltpu.VMEM((ctx_n, 2 * tokens, LANES), BF16),
             pltpu.VMEM((ctx_n, 2 * tokens, LANES), BF16),
             pltpu.VMEM((ctx_n, tokens, LANES), BF16),
-            pltpu.VMEM((kvh_n, tokens, LANES), F32),
-            pltpu.VMEM((kvh_n, tokens, LANES), F32),
+            pltpu.VMEM((kvh_n, tokens, LANES), BF16),
+            pltpu.VMEM((kvh_n, tokens, LANES), BF16),
             pltpu.VMEM((kvh_n, ctx_n, 1, LANES), F32),
-            pltpu.VMEM((2, ctx_n, x_n, tokens, LANES), BF16),
-            pltpu.VMEM((2, ctx_n, x_n, tokens, LANES), F32),
-            pltpu.VMEM((2, ctx_n, x_n, tokens, LANES), BF16),
-            pltpu.VMEM((ctx_n, x_n, tokens, LANES), BF16),
-            pltpu.VMEM((ctx_n, x_n, tokens, LANES), BF16),
+            pltpu.VMEM((2, chips, tokens, LANES), BF16),
+            pltpu.VMEM((2, chips, tokens, LANES), F32),
+            pltpu.VMEM((2, chips, tokens, LANES), BF16),
             pltpu.VMEM((chips, tokens, LANES), BF16),
+            pltpu.VMEM((chips, tokens, LANES), BF16),
+            pltpu.VMEM((chips, tokens, LANES), BF16),
+            dma((5,)),
             dma((batch,)),
             dma((4,)),
             dma((9,)),
             dma((6,)),
-            dma((classes,)),
-            dma((classes,)),
-            dma((classes,)),
-            dma((classes,)),
+            dma((2,)),
+            dma((planes // 2 + ctx_n // planes // 2,)),
+            dma((group_n,)),
+            dma((group_n,)),
+            dma((group_n,)),
         ],
         compiler_params=pltpu.CompilerParams(
             collective_id=0, has_side_effects=True, vmem_limit_bytes=56 * 2**20

time: 47.3 us -> 43.7 us (0.924)
  Pallas kernels: 45.8 us -> 43 us
  local copies, waits for them, and re-layouts: 1.28 us -> 0.6 us
    pallas_call x1, Pallas kernels: 45.8 us -> 43 us  [per_device(): pl.pallas_call(functools.partial(layer_kernel, (ctx_n, kvh_n, planes, ste...]
    unnamed x1, local copies, waits for them, and re-layouts: 1.28 us -> 0.6 us
where the time goes in v3:
time: 43.7 us; the launch traced here: 43.6 us
  Pallas kernels  43 us (98%)
  local copies, waits for them, and re-layouts  0.6 us (1%)
    pallas_call x1, Pallas kernels, per_device(): pl.pallas_call(functools.partial(layer_kernel, (ctx_n, kvh_n, planes, ste...  43 us

profile of v3, /device:TPU:1, one launch (start us, length us, event | category | flops | bytes accessed | tf_op | source)
XLA Modules:
  0.0 43.6 jit_solution(514085806445511167)
XLA Ops:
  0.0 43.0 %layer.1 = bf16[16,128]{1,0:T(8,128)(2,1)S(1)} custom-call(bf16[4,4,2048]{2,1,0:T(4,128)(2,1)} %query_hbm.1, bf16[2,16,128]{2,1,0:T(8,128)(2,1)} %bitcast.7, s32[4]{0:T(128)} %lengths_hbm.1, bf16[16,128]{1,0:T(8,128)(2,1)} %bitcast.8, f32[1,128]{1,0:T(1,128)} %bitcast.9, bf16[2,4,1024,128]{3,2,1,0:T(8,128)(2,1)} %bitcast.6, bf16[2048,1024]{1,0:T(8,128)(2,1)} %out_hbm.1, ...), custom_call_target="tpu_custom_call" | custom-call | tf_op jit(solution)/shard_map/layer/pallas_call | solution.py:457
  43.0 0.6 %copy.12 = bf16[4,4,128]{2,1,0:T(4,128)(2,1)} copy(bf16[4,4,128]{2,1,0:T(4,128)(2,1)S(1)} %bitcast.5) | data formatting | bytes 8192

commit v4 on v3

--- a/solution.py
+++ b/solution.py
@@ -57,6 +57,8 @@
     out_w,
     gate_up_w,
     down_w,
+    gate_up_other,
+    down_other,
     queries,
     numer,
     stats,
@@ -67,9 +69,10 @@
     proj_in,
     gains,
     feats,
-    half_wide,
-    half_msg,
-    half_in,
+    halves_out,
+    halves_in,
+    squares_out,
+    squares_in,
     pair_msg,
     down_in,
     input_sem,
@@ -80,8 +83,6 @@
     part_sem,
     head_sem,
     feat_sem,
-    relay_sem,
-    half_sem,
 ):
     ctx_n, kvh_n, planes, steps, batch = dims
     x_n = kvh_n // 2
@@ -239,12 +240,29 @@
             (to, kvh),
         )
     att_in[0] = att_msg[ctx]
+
     gains[kvh, ctx] = gain[...]
 
     @pl.loop(1, ctx_n)
     def _(i):
         to = lax.rem(ctx + i, ctx_n)
         send(gains.at[kvh, ctx], gains.at[kvh, ctx], send_sem.at[1], recv_sem.at[1], (to, kvh))
+
+    def side(n, which):
+        at_ctx, at_x = chip_at[n]
+        return pl.ds(pl.multiple_of(((at_ctx * x_n + at_x) * 2 + which) * LANES, LANES), LANES)
+
+    def hand_over(src, dst, at_send, at_recv):
+        for n in range(chips):
+            send(
+                src.at[:, side(n, 1 - core)],
+                dst.at[:, n * LANES : (n + 1) * LANES],
+                at_send,
+                at_recv,
+                partner,
+            )
+
+    hand_over(gate_hbm, gate_up_other.at[0:units], send_sem.at[9], recv_sem.at[6])
 
     def merged(low, high):
         parts = [att_in[i, tokens : 2 * tokens, :].astype(F32) for i in range(low, high)]
@@ -277,6 +295,9 @@
             head_sem.at[max(hops[n] - 1, 0)],
             (ctx_at[n], kvh),
         )
+
+    hand_over(up_hbm, gate_up_other.at[units : 2 * units], send_sem.at[10], recv_sem.at[7])
+    hand_over(down_hbm, down_other, send_sem.at[11], recv_sem.at[8])
 
     drain(gains.at[0, 0 : ctx_n - 1], recv_sem.at[1])
 
@@ -318,86 +339,67 @@
     for k in range(kvh_n):
         carried = carried + proj_in[k].astype(F32)
     carried = carried.astype(BF16)
-    feats[core, 0] = carried
+    feats[0] = carried
 
     far_hops = cuts[-1][0]
     outward = sorted(range(1, chips), key=lambda n: (chip_hops[n] < far_hops, n))
     for n in outward:
         to_ctx, to_x = chip_at[n]
         send(
-            feats.at[core, 0],
-            feats.at[core, chip_opposite[n]],
+            feats.at[0],
+            feats.at[chip_opposite[n]],
             send_sem.at[5],
             feat_sem.at[group_at[n]],
             (to_ctx, to_x * 2 + core),
         )
 
-    width = 2 * LANES
-    products = jnp.zeros((tokens, 2 * units), F32)
-    squares = jnp.zeros((tokens, LANES), F32)
-
-    def chip_columns(n):
-        at_ctx, at_x = chip_at[n]
-        return pl.ds(pl.multiple_of((at_ctx * x_n + at_x) * width, width), width)
-
-    def relay(g):
-        low, high = groups[g]
-        drain(feats.at[core, low : high - 1 if g == 0 else high], feat_sem.at[g])
-        block = feats.at[core, low:high]
-        send(block, block, send_sem.at[6], relay_sem.at[g], partner)
-
     weight_copies[1].wait()
     weight_copies[2].wait()
-    relay(0)
+    drain(gate_up_other.at[0:units], recv_sem.at[6])
+    drain(gate_up_other.at[units : 2 * units], recv_sem.at[7])
+    products = jnp.zeros((tokens, 2 * units), F32)
+    products_other = jnp.zeros((tokens, 2 * units), F32)
+    squares = jnp.zeros((tokens, LANES), F32)
     for g, (low, high) in enumerate(groups):
-        if g + 1 < len(groups):
-            relay(g + 1)
-        drain(feats.at[1 - core, low:high], relay_sem.at[g])
+        drain(feats.at[low : high - 1 if g == 0 else high], feat_sem.at[g])
         pieces = []
         for n in range(low, high):
             at_ctx, at_x = chip_at[n]
-            for c in range(2):
-                piece = feats[c, n].astype(F32)
-                squares = squares + piece * piece
-                pieces.append((piece * gains[at_x * 2 + c, at_ctx]).astype(BF16))
+            piece = feats[n].astype(F32)
+            squares = squares + piece * piece
+            pieces.append((piece * gains[at_x * 2 + core, at_ctx]).astype(BF16))
         rows = jnp.concatenate(pieces, axis=1)
-        matching = jnp.concatenate(
-            [gate_up_w[:, chip_columns(n)] for n in range(low, high)], axis=1
-        )
+        matching = jnp.concatenate([gate_up_w[:, side(n, core)] for n in range(low, high)], axis=1)
         products = products + dot_rows(rows, matching)
+        matching = gate_up_other[:, low * LANES : high * LANES]
+        products_other = products_other + dot_rows(rows, matching)
+    halves_out[0] = products
+    halves_out[1] = products_other
+    squares_out[...] = squares
+    send(halves_out, halves_in, send_sem.at[6], recv_sem.at[9], partner)
+    send(squares_out, squares_in, send_sem.at[7], recv_sem.at[10], partner)
+    drain(halves_in, recv_sem.at[9])
+    drain(squares_in, recv_sem.at[10])
+    squares = squares + squares_in[...]
     mean_square = jnp.sum(squares, axis=1, keepdims=True) / (chips * 2 * LANES)
-    products = products * lax.rsqrt(mean_square + EPSILON)
-    gate = products[:, 0:units]
-    up = products[:, units : 2 * units]
-    hidden = (gate / (1.0 + jnp.exp(-gate)) * up).astype(BF16)
+    inverse = lax.rsqrt(mean_square + EPSILON)
+
+    def activated(total):
+        gate = total[:, 0:units] * inverse
+        up = total[:, units : 2 * units] * inverse
+        return (gate / (1.0 + jnp.exp(-gate)) * up).astype(BF16)
+
+    hidden = activated(products + halves_in[1])
+    hidden_other = activated(products_other + halves_in[0])
 
     weight_copies[3].wait()
-    groups = groups[:1:-1] + [(0, groups[1][1])]
-
-    def halves(g):
-        low, high = groups[g]
-        matching = jnp.concatenate([down_w[:, chip_columns(n)] for n in range(low, high)], axis=1)
+    drain(down_other, recv_sem.at[8])
+    for low, high in groups[:1:-1] + [(0, groups[1][1])]:
+        matching = jnp.concatenate([down_w[:, side(n, core)] for n in range(low, high)], axis=1)
         block = dot(hidden, matching)
-        for n in range(low, high):
-            for c in range(2):
-                at = (n - low) * width + c * LANES
-                piece = block[:, at : at + LANES]
-                half_wide[c, n] = piece
-                half_msg[c, n] = piece.astype(BF16)
-        send(
-            half_msg.at[1 - core, low:high],
-            half_in.at[low:high],
-            send_sem.at[7],
-            half_sem.at[g],
-            partner,
-        )
-
-    def spread(g):
-        low, high = groups[g]
-        drain(half_in.at[low:high], half_sem.at[g])
-        pair_msg[low:high] = (half_wide[core, low:high] + half_in[low:high].astype(F32)).astype(
-            BF16
-        )
+        block = block + dot(hidden_other, down_other[:, low * LANES : high * LANES])
+        for n in range(high - 1, low - 1, -1):
+            pair_msg[n] = block[:, (n - low) * LANES : (n - low + 1) * LANES].astype(BF16)
         for n in range(high - 1, max(low, 1) - 1, -1):
             to_ctx, to_x = chip_at[n]
             send(
@@ -407,12 +409,6 @@
                 recv_sem.at[5],
                 (to_ctx, to_x * 2 + core),
             )
-
-    for g in range(len(groups)):
-        halves(g)
-        if g >= 1:
-            spread(g - 1)
-    spread(len(groups) - 1)
     down_in[0] = pair_msg[0]
     drain(down_in.at[0 : chips - 1], recv_sem.at[5])
     final = carried.astype(F32) + jnp.sum(down_in[...].astype(F32), axis=0)
@@ -424,9 +420,12 @@
     drain(gains.at[0 : kvh_n - 1], send_sem.at[3])
     drain(proj_in.at[0 : kvh_n - 1], send_sem.at[4])
     drain(down_in.at[0 : chips - 1], send_sem.at[5])
-    drain(feats.at[0], send_sem.at[6])
-    drain(half_in, send_sem.at[7])
+    drain(halves_in, send_sem.at[6])
+    drain(squares_in, send_sem.at[7])
     drain(down_in.at[0 : chips - 1], send_sem.at[8])
+    drain(down_other, send_sem.at[9])
+    drain(down_other, send_sem.at[10])
+    drain(down_other, send_sem.at[11])
 
 
 def per_device(ctx_n, kvh_n, planes, *arguments):
@@ -469,6 +468,8 @@
             pltpu.VMEM(out_weight.shape, BF16),
             pltpu.VMEM((2 * units, gate_weight.shape[1]), BF16),
             pltpu.VMEM(down_weight.shape, BF16),
+            pltpu.VMEM((2 * units, chips * LANES), BF16),
+            pltpu.VMEM((units, chips * LANES), BF16),
             pltpu.VMEM((ctx_n * tokens, LANES), F32),
             pltpu.VMEM((ctx_n * tokens, LANES), F32),
             pltpu.VMEM((ctx_n * tokens, LANES), F32),
@@ -478,21 +479,20 @@
             pltpu.VMEM((kvh_n, tokens, LANES), BF16),
             pltpu.VMEM((kvh_n, tokens, LANES), BF16),
             pltpu.VMEM((kvh_n, ctx_n, 1, LANES), F32),
-            pltpu.VMEM((2, chips, tokens, LANES), BF16),
-            pltpu.VMEM((2, chips, tokens, LANES), F32),
-            pltpu.VMEM((2, chips, tokens, LANES), BF16),
             pltpu.VMEM((chips, tokens, LANES), BF16),
+            pltpu.VMEM((2, tokens, 2 * units), F32),
+            pltpu.VMEM((2, tokens, 2 * units), F32),
+            pltpu.VMEM((tokens, LANES), F32),
+            pltpu.VMEM((tokens, LANES), F32),
             pltpu.VMEM((chips, tokens, LANES), BF16),
             pltpu.VMEM((chips, tokens, LANES), BF16),
             dma((5,)),
             dma((batch,)),
             dma((4,)),
-            dma((9,)),
-            dma((6,)),
+            dma((12,)),
+            dma((11,)),
             dma((2,)),
             dma((planes // 2 + ctx_n // planes // 2,)),
-            dma((group_n,)),
-            dma((group_n,)),
             dma((group_n,)),
         ],
         compiler_params=pltpu.CompilerParams(

time: 43.7 us -> 41.6 us (0.952)
  Pallas kernels: 43 us -> 40.9 us
    pallas_call x1, Pallas kernels: 43 us -> 40.9 us  [per_device(): pl.pallas_call(functools.partial(layer_kernel, (ctx_n, kvh_n, planes, ste...]
where the time goes in v4:
time: 41.6 us; the launch traced here: 41.5 us
  Pallas kernels  40.9 us (98%)
  local copies, waits for them, and re-layouts  0.6 us (1%)
    pallas_call x1, Pallas kernels, per_device(): pl.pallas_call(functools.partial(layer_kernel, (ctx_n, kvh_n, planes, ste...  40.9 us

profile of v4, /device:TPU:1, one launch (start us, length us, event | category | flops | bytes accessed | tf_op | source)
XLA Modules:
  0.0 41.5 jit_solution(936133119145382138)
XLA Ops:
  0.0 40.9 %layer.1 = bf16[16,128]{1,0:T(8,128)(2,1)S(1)} custom-call(bf16[4,4,2048]{2,1,0:T(4,128)(2,1)} %query_hbm.1, bf16[2,16,128]{2,1,0:T(8,128)(2,1)} %bitcast.7, s32[4]{0:T(128)} %lengths_hbm.1, bf16[16,128]{1,0:T(8,128)(2,1)} %bitcast.8, f32[1,128]{1,0:T(1,128)} %bitcast.9, bf16[2,4,1024,128]{3,2,1,0:T(8,128)(2,1)} %bitcast.6, bf16[2048,1024]{1,0:T(8,128)(2,1)} %out_hbm.1, ...), custom_call_target="tpu_custom_call" | custom-call | tf_op jit(solution)/shard_map/layer/pallas_call | solution.py:456
  40.9 0.6 %copy.12 = bf16[4,4,128]{2,1,0:T(4,128)(2,1)} copy(bf16[4,4,128]{2,1,0:T(4,128)(2,1)S(1)} %bitcast.5) | data formatting | bytes 8192

commit v5 on v4

--- a/solution.py
+++ b/solution.py
@@ -297,7 +297,6 @@
         )
 
     hand_over(up_hbm, gate_up_other.at[units : 2 * units], send_sem.at[10], recv_sem.at[7])
-    hand_over(down_hbm, down_other, send_sem.at[11], recv_sem.at[8])
 
     drain(gains.at[0, 0 : ctx_n - 1], recv_sem.at[1])
 
@@ -333,6 +332,7 @@
         send(proj_msg.at[to], proj_in.at[kvh], send_sem.at[4], recv_sem.at[4], (ctx, to))
 
     proj_in[kvh] = proj_msg[kvh]
+    hand_over(down_hbm, down_other, send_sem.at[11], recv_sem.at[8])
     drain(gains.at[0 : kvh_n - 1], recv_sem.at[3])
     drain(proj_in.at[0 : kvh_n - 1], recv_sem.at[4])
     carried = residual[...].astype(F32)
@@ -341,9 +341,7 @@
     carried = carried.astype(BF16)
     feats[0] = carried
 
-    far_hops = cuts[-1][0]
-    outward = sorted(range(1, chips), key=lambda n: (chip_hops[n] < far_hops, n))
-    for n in outward:
+    for n in range(1, chips):
         to_ctx, to_x = chip_at[n]
         send(
             feats.at[0],

time: 41.6 us -> 41.3 us (level)
  no operation moved by 1% of the time
where the time goes in v5:
time: 41.3 us; the launch traced here: 41.2 us
  Pallas kernels  40.6 us (98%)
  local copies, waits for them, and re-layouts  0.6 us (1%)
    pallas_call x1, Pallas kernels, per_device(): pl.pallas_call(functools.partial(layer_kernel, (ctx_n, kvh_n, planes, ste...  40.6 us

profile of v5, /device:TPU:1, one launch (start us, length us, event | category | flops | bytes accessed | tf_op | source)
XLA Modules:
  0.0 41.2 jit_solution(1914610844323312889)
XLA Ops:
  0.0 40.6 %layer.1 = bf16[16,128]{1,0:T(8,128)(2,1)S(1)} custom-call(bf16[4,4,2048]{2,1,0:T(4,128)(2,1)} %query_hbm.1, bf16[2,16,128]{2,1,0:T(8,128)(2,1)} %bitcast.7, s32[4]{0:T(128)} %lengths_hbm.1, bf16[16,128]{1,0:T(8,128)(2,1)} %bitcast.8, f32[1,128]{1,0:T(1,128)} %bitcast.9, bf16[2,4,1024,128]{3,2,1,0:T(8,128)(2,1)} %bitcast.6, bf16[2048,1024]{1,0:T(8,128)(2,1)} %out_hbm.1, ...), custom_call_target="tpu_custom_call" | custom-call | tf_op jit(solution)/shard_map/layer/pallas_call | solution.py:454
  40.6 0.6 %copy.12 = bf16[4,4,128]{2,1,0:T(4,128)(2,1)} copy(bf16[4,4,128]{2,1,0:T(4,128)(2,1)S(1)} %bitcast.5) | data formatting | bytes 8192

commit v6 on v5

--- a/solution.py
+++ b/solution.py
@@ -230,7 +230,7 @@
 
     pl.semaphore_wait(barrier, ctx_n + kvh_n - 2)
 
-    for n in range(1, ctx_n):
+    for n in range(ctx_n - 1, 0, -1):
         to = ctx_at[n]
         send(
             att_msg.at[to],
@@ -287,7 +287,7 @@
         numerator = factor * numerator + factor2 * numerator2
     heads[0] = (numerator / denominator).astype(BF16)
 
-    for n in range(1, ctx_n):
+    for n in range(ctx_n - 1, 0, -1):
         send(
             heads.at[0],
             heads.at[opposite[n]],

time: 41.3 us -> 40.9 us (level)
  Pallas kernels: 40.6 us -> 40.1 us
    pallas_call x1, Pallas kernels: 40.6 us -> 40.1 us  [per_device(): pl.pallas_call(functools.partial(layer_kernel, (ctx_n, kvh_n, planes, ste...]
where the time goes in v6:
time: 40.9 us; the launch traced here: 40.7 us
  Pallas kernels  40.1 us (98%)
  local copies, waits for them, and re-layouts  0.6 us (1%)
    pallas_call x1, Pallas kernels, per_device(): pl.pallas_call(functools.partial(layer_kernel, (ctx_n, kvh_n, planes, ste...  40.1 us

profile of v6, /device:TPU:1, one launch (start us, length us, event | category | flops | bytes accessed | tf_op | source)
XLA Modules:
  0.0 40.7 jit_solution(15017858767847765980)
XLA Ops:
  0.0 40.1 %layer.1 = bf16[16,128]{1,0:T(8,128)(2,1)S(1)} custom-call(bf16[4,4,2048]{2,1,0:T(4,128)(2,1)} %query_hbm.1, bf16[2,16,128]{2,1,0:T(8,128)(2,1)} %bitcast.7, s32[4]{0:T(128)} %lengths_hbm.1, bf16[16,128]{1,0:T(8,128)(2,1)} %bitcast.8, f32[1,128]{1,0:T(1,128)} %bitcast.9, bf16[2,4,1024,128]{3,2,1,0:T(8,128)(2,1)} %bitcast.6, bf16[2048,1024]{1,0:T(8,128)(2,1)} %out_hbm.1, ...), custom_call_target="tpu_custom_call" | custom-call | tf_op jit(solution)/shard_map/layer/pallas_call | solution.py:454
  40.1 0.6 %copy.12 = bf16[4,4,128]{2,1,0:T(4,128)(2,1)} copy(bf16[4,4,128]{2,1,0:T(4,128)(2,1)S(1)} %bitcast.5) | data formatting | bytes 8192
